TPU v7x, 32 devices: a whole 2x2x4 slice. The times are simulated.
32 devices in a mesh: section: 2 (over x), dp: 4 (over z), tensor: 4 (over y, core).
Axes of the slice: x: 2, y: 2, z: 4, core: 2. Of those that a mesh axis runs over, the one named last changes fastest.
Arguments:
- images: bfloat16 [16, 196, 512], P('dp'), may hold values from -6 to 6
- out_grad: bfloat16 [16, 196, 512], P('dp'), may hold values from -6 to 6
- ln_gain: float32 [2, 2, 512], P('section'), may hold values from 0.5 to 1.5
- ln_bias: float32 [2, 2, 512], P('section'), may hold values from -2 to 2
- qkv_weight: bfloat16 [2, 3, 512, 512], P('section', None, None, 'tensor'), may hold values from -0.25 to 0.25
- qv_bias: float32 [2, 2, 512], P('section', None, 'tensor'), may hold values from -2 to 2
- pos_table: float32 [2, 169, 16], P('section', None, 'tensor'), may hold values from -4 to 4
- proj_weight: bfloat16 [2, 512, 512], P('section', 'tensor'), may hold values from -0.75 to 0.75
- out_bias: float32 [2, 2, 512], P('section'), may hold values from -2 to 2
- fc1_weight: bfloat16 [2, 512, 2048], P('section', None, 'tensor'), may hold values from -0.25 to 0.25
- fc1_bias: float32 [2, 2048], P('section', 'tensor'), may hold values from -2 to 2
- fc2_weight: bfloat16 [2, 2048, 512], P('section', 'tensor'), may hold values from -0.1875 to 0.1875
- rel_index: int32 [49, 49], replicated, may hold values from 0 to 168, as said below
- regions: int32 [14, 14], replicated, may hold values from 0 to 8, as said below
Outputs:
- section_out: bfloat16 [2, 16, 196, 512], P('section', 'dp')
- input_grad: float32 [2, 16, 196, 512], P('section', 'dp')
- grad_ln_gain: float32 [2, 2, 512], P('section')
- grad_ln_bias: float32 [2, 2, 512], P('section')
- grad_qkv_weight: float32 [2, 3, 512, 512], P('section', None, None, 'tensor')
- grad_qv_bias: float32 [2, 2, 512], P('section', None, 'tensor')
- grad_pos_table: float32 [2, 169, 16], P('section', None, 'tensor')
- grad_proj_weight: float32 [2, 512, 512], P('section', 'tensor')
- grad_out_bias: float32 [2, 2, 512], P('section')
- grad_fc1_weight: float32 [2, 512, 2048], P('section', None, 'tensor')
- grad_fc1_bias: float32 [2, 2048], P('section', 'tensor')
- grad_fc2_weight: float32 [2, 2048, 512], P('section', 'tensor')
Inputs may be any that keep to these rules, and one draw needn't show every extreme that they name: rel_index[a, c] = p((row(a) - row(c) + 6) * 13 + column(a) - column(c) + 6) for a one-to-one map p of 0 to 168 onto itself, with row and column of a token inside its window. regions[i, j] = 3 * u(i) + v(j), where u and v split 0 to 13 into three nonempty runs of consecutive places numbered 0, 1, 2.
All inputs are finite; a program needn't handle non-finite values.
Results may differ from a plain program's by a relative error of at most 0.028.
Values may be sent and summed in bfloat16 or wider, within the bound.
No kernel may reach another device: no remote copies, remote signals or barrier semaphores. Data moves between devices by JAX's collectives and lax.ppermute only.
A program may use at most 128 MiB of HBM per device.

v0:
```python
import jax
import jax.numpy as jnp
from jax import lax
from jax.sharding import PartitionSpec as P

D = 512
HEAD_DIM = 32
WIN = 7
SIDE = 14
SHIFT = 3
MICRO = 2
PIX = 196
WTOK = 49
REL = 169


epsilon = 1e-05
highest = lax.Precision.HIGHEST


def from_behind(array, axis, by):
    devices = lax.axis_size(axis)
    pairs = [(i, i + by) for i in range(devices) if 0 <= i + by < devices]
    return lax.ppermute(array, axis, pairs)


def layer_norm(values, gain, offset):
    center = values - jnp.mean(values, -1, keepdims=True)
    spread = jnp.mean(center * center, -1, keepdims=True)
    return center * lax.rsqrt(spread + epsilon) * gain + offset


def to_tiles(lattice):
    amount = lattice.shape[0]
    stripes = SIDE // WIN
    shaped = lattice.reshape(amount, stripes, WIN, stripes, WIN, lattice.shape[-1])
    return shaped.transpose(0, 1, 3, 2, 4, 5).reshape(
        amount, stripes * stripes, WIN * WIN, lattice.shape[-1]
    )


def from_tiles(windowed):
    amount = windowed.shape[0]
    stripes = SIDE // WIN
    shaped = windowed.reshape(amount, stripes, stripes, WIN, WIN, windowed.shape[-1])
    return shaped.transpose(0, 1, 3, 2, 4, 5).reshape(amount, SIDE * SIDE, windowed.shape[-1])


def region_mask(regions):
    stripes = SIDE // WIN
    tiled = (
        regions.reshape(stripes, WIN, stripes, WIN)
        .transpose(0, 2, 1, 3)
        .reshape(stripes * stripes, WIN * WIN)
    )
    return jnp.where(tiled[:, :, None] != tiled[:, None, :], -100.0, 0.0).astype(jnp.float32)


def roll_grid(inputs, shifted, direction):
    amount = inputs.shape[0]
    lattice = inputs.reshape(amount, SIDE, SIDE, inputs.shape[-1])
    rolled = jnp.roll(lattice, (direction * SHIFT, direction * SHIFT), (1, 2))
    return jnp.where(shifted, rolled, lattice).reshape(amount, SIDE * SIDE, inputs.shape[-1])


def head_split(packed):
    return packed.reshape(packed.shape[:-1] + (packed.shape[-1] // HEAD_DIM, HEAD_DIM))


def attention_scores(split, bias_heads, region_bias):
    scores = jnp.einsum(
        "nwahd,nwbhd->nwhab", split[0], split[1], preferred_element_type=jnp.float32
    )
    return scores * HEAD_DIM ** (-0.5) + bias_heads[None, None] + region_bias[None, :, None]


def data_sum(grads):
    return (
        lax.psum(grads[0].astype(jnp.bfloat16), "dp").astype(jnp.float32),
        lax.psum(grads[1].astype(jnp.bfloat16), "dp").astype(jnp.float32),
        lax.psum(grads[2].astype(jnp.bfloat16), "dp").astype(jnp.float32),
        lax.psum(grads[3].astype(jnp.bfloat16), "dp").astype(jnp.float32),
        lax.psum(grads[4].astype(jnp.bfloat16), "dp").astype(jnp.float32),
        lax.psum(grads[5].astype(jnp.bfloat16), "dp").astype(jnp.float32),
        lax.psum(grads[6].astype(jnp.bfloat16), "dp").astype(jnp.float32),
        lax.psum(grads[7].astype(jnp.bfloat16), "dp").astype(jnp.float32),
        lax.psum(grads[8].astype(jnp.bfloat16), "dp").astype(jnp.float32),
        lax.psum(grads[9].astype(jnp.bfloat16), "dp").astype(jnp.float32),
    )


def block_forward(inputs, params, setup):
    norm_gains, norm_shifts, qkv_w, qv_b, proj_w, out_b, fc1_w, fc1_b, fc2_w = params
    bias_heads, region_bias, shifted = setup
    windowed = to_tiles(roll_grid(inputs, shifted, -1))
    normed = layer_norm(windowed, norm_gains[0], norm_shifts[0]).astype(jnp.bfloat16)
    projected = jnp.einsum("nwtc,jce->jnwte", normed, qkv_w, preferred_element_type=jnp.float32)
    bias_rows = jnp.stack([qv_b[0], jnp.zeros_like(qv_b[0]), qv_b[1]])
    packed = (projected + bias_rows[:, None, None, None, :]).astype(jnp.bfloat16)
    split = head_split(packed)
    scores = attention_scores(split, bias_heads, region_bias)
    top_score = jnp.max(scores, -1, keepdims=True)
    exp_scores = jnp.exp(scores - top_score)
    score_total = jnp.sum(exp_scores, -1, keepdims=True)
    log_total = top_score + jnp.log(score_total)
    soft_low = (exp_scores / score_total).astype(jnp.bfloat16)
    context = jnp.einsum(
        "nwhab,nwbhd->nwahd", soft_low, split[2], preferred_element_type=jnp.float32
    )
    context = context.reshape(windowed.shape[:-1] + (packed.shape[-1],)).astype(jnp.bfloat16)
    part_sum = jnp.einsum("nwte,ec->nwtc", context, proj_w, preferred_element_type=jnp.float32)
    branch = lax.psum(part_sum.astype(jnp.bfloat16), "tensor").astype(jnp.float32) + out_b[0]
    middle = windowed + branch
    normed2 = layer_norm(middle, norm_gains[1], norm_shifts[1]).astype(jnp.bfloat16)
    preact = jnp.einsum("nwtc,cf->nwtf", normed2, fc1_w, preferred_element_type=jnp.float32) + fc1_b
    hidden = jax.nn.gelu(preact, approximate=False).astype(jnp.bfloat16)
    part_second = jnp.einsum("nwtf,fc->nwtc", hidden, fc2_w, preferred_element_type=jnp.float32)
    result = (
        middle + lax.psum(part_second.astype(jnp.bfloat16), "tensor").astype(jnp.float32) + out_b[1]
    )
    output = roll_grid(from_tiles(result), shifted, 1)
    return (output, (windowed, normed, packed, log_total, context, middle, normed2, preact, hidden))


def block_backward(upstream, saved, params, setup, onehot):
    norm_gains, norm_shifts, qkv_w, qv_b, proj_w, out_b, fc1_w, fc1_b, fc2_w = params
    bias_heads, region_bias, shifted = setup
    windowed, normed, packed, log_total, context, middle, normed2, preact, hidden = saved
    grad_tiles = to_tiles(roll_grid(upstream, shifted, -1))
    grad_mlp = grad_tiles.astype(jnp.bfloat16)
    mlp_bias_grad = jnp.sum(grad_mlp, (0, 1, 2), dtype=jnp.float32)
    fc2_grad = jnp.einsum("nwtf,nwtc->fc", hidden, grad_mlp, preferred_element_type=jnp.float32)
    grad_hidden = jnp.einsum("nwtc,fc->nwtf", grad_mlp, fc2_w, preferred_element_type=jnp.float32)
    gelu_pull = jax.vjp(lambda inner: jax.nn.gelu(inner, approximate=False), preact)[1]
    grad_preact = gelu_pull(grad_hidden)[0].astype(jnp.bfloat16)
    fc1_bias_grad = jnp.sum(grad_preact, (0, 1, 2), dtype=jnp.float32)
    fc1_grad = jnp.einsum("nwtc,nwtf->cf", normed2, grad_preact, preferred_element_type=jnp.float32)
    partial_second = jnp.einsum(
        "nwtf,cf->nwtc", grad_preact, fc1_w, preferred_element_type=jnp.float32
    )
    grad_normed2 = lax.psum(partial_second.astype(jnp.bfloat16), "tensor").astype(jnp.float32)
    second_pull = jax.vjp(layer_norm, middle, norm_gains[1], norm_shifts[1])[1]
    grad_middle_norm, gain2_grad, shift2_grad = second_pull(grad_normed2)
    grad_middle = grad_tiles + grad_middle_norm
    grad_branch = grad_middle.astype(jnp.bfloat16)
    proj_bias_grad = jnp.sum(grad_branch, (0, 1, 2), dtype=jnp.float32)
    proj_grad = jnp.einsum(
        "nwte,nwtc->ec", context, grad_branch, preferred_element_type=jnp.float32
    )
    grad_context = jnp.einsum(
        "nwtc,ec->nwte", grad_branch, proj_w, preferred_element_type=jnp.float32
    ).astype(jnp.bfloat16)
    split = head_split(packed)
    scores = attention_scores(split, bias_heads, region_bias)
    soft = jnp.exp(scores - log_total)
    soft_low = soft.astype(jnp.bfloat16)
    grad_heads = grad_context.reshape(split.shape[1:])
    grad_values = jnp.einsum(
        "nwhab,nwahd->nwbhd", soft_low, grad_heads, preferred_element_type=jnp.float32
    )
    grad_soft = jnp.einsum(
        "nwahd,nwbhd->nwhab", grad_heads, split[2], preferred_element_type=jnp.float32
    )
    grad_scores = (soft * (grad_soft - jnp.sum(grad_soft * soft, -1, keepdims=True))).astype(
        jnp.bfloat16
    )
    score_sums = jnp.sum(grad_scores, (0, 1), dtype=jnp.float32)
    head_count = score_sums.shape[0]
    table_grad = jnp.dot(
        onehot.T, score_sums.transpose(1, 2, 0).reshape(-1, head_count), precision=highest
    )
    factor = HEAD_DIM ** (-0.5)
    grad_queries = (
        jnp.einsum("nwhab,nwbhd->nwahd", grad_scores, split[1], preferred_element_type=jnp.float32)
        * factor
    )
    grad_keys = (
        jnp.einsum("nwhab,nwahd->nwbhd", grad_scores, split[0], preferred_element_type=jnp.float32)
        * factor
    )
    grad_packed = (
        jnp.stack([grad_queries, grad_keys, grad_values]).reshape(packed.shape).astype(jnp.bfloat16)
    )
    qv_grad = jnp.stack(
        [
            jnp.sum(grad_packed[0], (0, 1, 2), dtype=jnp.float32),
            jnp.sum(grad_packed[2], (0, 1, 2), dtype=jnp.float32),
        ]
    )
    qkv_grad = jnp.einsum(
        "nwtc,jnwte->jce", normed, grad_packed, preferred_element_type=jnp.float32
    )
    partial_first = jnp.einsum(
        "jnwte,jce->nwtc", grad_packed, qkv_w, preferred_element_type=jnp.float32
    )
    grad_normed = lax.psum(partial_first.astype(jnp.bfloat16), "tensor").astype(jnp.float32)
    first_pull = jax.vjp(layer_norm, windowed, norm_gains[0], norm_shifts[0])[1]
    grad_windowed, gain1_grad, shift1_grad = first_pull(grad_normed)
    down_share = grad_middle + grad_windowed
    gain_grads = jnp.stack([gain1_grad, gain2_grad])
    shift_grads = jnp.stack([shift1_grad, shift2_grad])
    downstream = roll_grid(from_tiles(down_share), shifted, 1)
    grads = (
        gain_grads,
        shift_grads,
        qkv_grad,
        qv_grad,
        table_grad,
        proj_grad,
        jnp.stack([proj_bias_grad, mlp_bias_grad]),
        fc1_grad,
        fc1_bias_grad,
        fc2_grad,
    )
    return (downstream, grads)


def local(
    images,
    out_grad,
    ln_gain,
    ln_bias,
    qkv_weight,
    qv_bias,
    pos_table,
    proj_weight,
    out_bias,
    fc1_weight,
    fc1_bias,
    fc2_weight,
    rel_index,
    regions,
):
    section = lax.axis_index("section")
    shifted = section == 1
    params = (
        ln_gain[0],
        ln_bias[0],
        qkv_weight[0],
        qv_bias[0],
        proj_weight[0],
        out_bias[0],
        fc1_weight[0],
        fc1_bias[0],
        fc2_weight[0],
    )
    pos_bias = pos_table[0]
    head_count = pos_bias.shape[-1]
    onehot = (rel_index.reshape(-1)[:, None] == jnp.arange(REL, dtype=jnp.int32)[None, :]).astype(
        jnp.float32
    )
    bias_heads = (
        jnp.dot(onehot, pos_bias, precision=highest)
        .reshape(WTOK, WTOK, head_count)
        .transpose(2, 0, 1)
    )
    region_bias = region_mask(regions) * shifted.astype(jnp.float32)
    setup = (bias_heads, region_bias, shifted)
    micro = MICRO
    per_batch = images.shape[0] // micro
    feed = images.reshape(micro, per_batch, PIX, D)
    cotangents = out_grad.reshape(micro, per_batch, PIX, D)
    outputs = []
    stored = []
    sent = jnp.zeros((per_batch, PIX, D), jnp.bfloat16)
    for moment in range(micro + 1):
        if moment == 0:
            arrived = jnp.zeros((per_batch, PIX, D), jnp.bfloat16)
        else:
            arrived = from_behind(sent, "section", 1)
        section_in = jnp.where(shifted, arrived, feed[min(moment, micro - 1)]).astype(jnp.float32)
        result, saved = block_forward(section_in, params, setup)
        sent = result.astype(jnp.bfloat16)
        outputs.append(sent)
        stored.append(saved)
    totals = None
    back_outs = []
    grad_sent = jnp.zeros((per_batch, PIX, D), jnp.bfloat16)
    for moment in range(micro + 1):
        if moment == 0:
            arrived = jnp.zeros((per_batch, PIX, D), jnp.bfloat16)
        else:
            arrived = from_behind(grad_sent, "section", -1)
        usable = jnp.where(shifted, float(moment < micro), float(moment >= 1))
        upstream = (
            jnp.where(shifted, cotangents[min(moment, micro - 1)], arrived).astype(jnp.float32)
            * usable
        )
        picked = jax.tree.map(
            lambda later, earlier: jnp.where(shifted, later, earlier),
            stored[min(moment + 1, micro)],
            stored[max(moment - 1, 0)],
        )
        saved = picked
        downstream, grads = block_backward(upstream, saved, params, setup, onehot)
        grad_sent = downstream.astype(jnp.bfloat16)
        back_outs.append(downstream)
        if totals is None:
            totals = grads
        else:
            totals = jax.tree.map(lambda left, right: left + right, totals, grads)
    totals = data_sum(totals)
    section_out = jnp.concatenate(
        [jnp.where(section == 0, outputs[index], outputs[index + 1]) for index in range(micro)]
    )[None]
    input_grad = jnp.concatenate(
        [jnp.where(section == 0, back_outs[index + 1], back_outs[index]) for index in range(micro)]
    )[None]
    return (section_out, input_grad) + tuple((summed[None] for summed in totals))


def solution(mesh):
    placed = (
        P("dp", None, None),
        P("dp", None, None),
        P("section", None, None),
        P("section", None, None),
        P("section", None, None, "tensor"),
        P("section", None, "tensor"),
        P("section", None, "tensor"),
        P("section", "tensor", None),
        P("section", None, None),
        P("section", None, "tensor"),
        P("section", "tensor"),
        P("section", "tensor", None),
        P(),
        P(),
    )
    return jax.shard_map(
        local,
        mesh=mesh,
        in_specs=placed,
        out_specs=(
            P("section", "dp", None, None),
            P("section", "dp", None, None),
            P("section", None, None),
            P("section", None, None),
            P("section", None, None, "tensor"),
            P("section", None, "tensor"),
            P("section", None, "tensor"),
            P("section", "tensor", None),
            P("section", None, None),
            P("section", None, "tensor"),
            P("section", "tensor"),
            P("section", "tensor", None),
        ),
        check_vma=False,
    )
```

profile of v0, /device:TPU:0, one launch (start us, length us, event | category | flops | bytes accessed | tf_op | source)
XLA Modules:
  0.0 655.7 jit_solution(3318536059488364724)
XLA Ops:
  20.3 35.5 %all-reduce.16.cloned.1.call-done = bf16[2,4,49,512]{3,2,1,0:T(8,128)(2,1)} async-done(((bf16[2,4,49,512]{3,2,1,0:T(8,128)(2,1)}), bf16[2,4,49,512]{3,2,1,0:T(8,128)(2,1)}) %all-reduce.16.cloned.1.call-update) | async-done | bytes 401424 | tf_op jit(solution)/shard_map/psum | solution.py:112
  64.9 33.0 %all-reduce.18.cloned.1.call-done = bf16[2,4,49,512]{3,2,1,0:T(8,128)(2,1)} async-done(((bf16[2,4,49,512]{3,2,1,0:T(8,128)(2,1)}), bf16[2,4,49,512]{3,2,1,0:T(8,128)(2,1)}) %all-reduce.18.cloned.1.call-update) | async-done | bytes 401424 | tf_op jit(solution)/shard_map/psum | solution.py:119
  101.2 3.4 collective-permute-start
  106.8 5.2 collective-permute-done
  126.6 30.9 %all-reduce.20.cloned.1.call-done = bf16[2,4,49,512]{3,2,1,0:T(8,128)(2,1)} async-done(((bf16[2,4,49,512]{3,2,1,0:T(8,128)(2,1)}), bf16[2,4,49,512]{3,2,1,0:T(8,128)(2,1)}) %all-reduce.20.cloned.1.call-update) | async-done | bytes 401424 | tf_op jit(solution)/shard_map/psum | solution.py:112
  158.8 3.0 fusion.313
  164.0 3.2 convert_reduce_fusion.8
  190.3 17.0 %all-reduce.32.cloned.1.call-done = (bf16[2,4,49,512]{3,2,1,0:T(8,128)(2,1)}, bf16[2,4,49,512]{3,2,1,0:T(8,128)(2,1)}) async-done(((bf16[2,4,49,512]{3,2,1,0:T(8,128)(2,1)}, bf16[2,4,49,512]{3,2,1,0:T(8,128)(2,1)}), (bf16[2,4,49,512]{3,2,1,0:T(8,128)(2,1)}, bf16[2,4,49,512]{3,2,1,0:T(8,128)(2,1)})) %all-reduce.32.cloned.1.call-update) | async-done | bytes 802832 | tf_op jit(solution)/shard_map/psum | solution.py:141
  214.3 4.4 collective-permute-start.1
  231.3 4.0 multiply_reduce_fusion.9
  310.4 4.4 fusion.309
  325.1 5.7 collective-permute-done.2
  334.7 3.2 convert_reduce_fusion.7
  339.9 2.7 convolution_bitcast_fusion.4
  347.7 30.8 %all-reduce.22.cloned.1.call-done = bf16[2,4,49,512]{3,2,1,0:T(8,128)(2,1)} async-done(((bf16[2,4,49,512]{3,2,1,0:T(8,128)(2,1)}), bf16[2,4,49,512]{3,2,1,0:T(8,128)(2,1)}) %all-reduce.22.cloned.1.call-update) | async-done | bytes 401424 | tf_op jit(solution)/shard_map/psum | solution.py:141
  408.7 30.8 %all-reduce.24.cloned.1.call-done = bf16[2,4,49,512]{3,2,1,0:T(8,128)(2,1)} async-done(((bf16[2,4,49,512]{3,2,1,0:T(8,128)(2,1)}), bf16[2,4,49,512]{3,2,1,0:T(8,128)(2,1)}) %all-reduce.24.cloned.1.call-update) | async-done | bytes 401424 | tf_op jit(solution)/shard_map/psum | solution.py:196
  452.0 7.0 %collective-permute-done.3 = bf16[2,196,512]{2,0,1:T(2,128)(2,1)S(1)} collective-permute-done((bf16[2,196,512]{2,0,1:T(2,128)(2,1)S(1)}, bf16[2,196,512]{2,0,1:T(2,128)(2,1)S(1)}, u32[]{:S(2)}, u32[]{:S(2)}) %collective-permute-start.3) | collective-permute-done | bytes 401440 | tf_op jit(solution)/shard_map/ppermute | solution.py:24
  463.1 3.2 convert_reduce_fusion.6
  468.3 2.6 convolution_bitcast_fusion.3
  478.4 26.6 %all-reduce.26.cloned.1.call-done = bf16[2,4,49,512]{3,2,1,0:T(8,128)(2,1)} async-done(((bf16[2,4,49,512]{3,2,1,0:T(8,128)(2,1)}), bf16[2,4,49,512]{3,2,1,0:T(8,128)(2,1)}) %all-reduce.26.cloned.1.call-update) | async-done | bytes 401424 | tf_op jit(solution)/shard_map/psum | solution.py:141
  540.3 27.6 %all-reduce.28.cloned.1.call-done = (bf16[2,4,49,512]{3,2,1,0:T(8,128)(2,1)}, bf16[2,4,49,512]{3,2,1,0:T(8,128)(2,1)}) async-done(((bf16[2,4,49,512]{3,2,1,0:T(8,128)(2,1)}, bf16[2,4,49,512]{3,2,1,0:T(8,128)(2,1)}), (bf16[2,4,49,512]{3,2,1,0:T(8,128)(2,1)}, bf16[2,4,49,512]{3,2,1,0:T(8,128)(2,1)})) %all-reduce.28.cloned.1.call-update) | async-done | bytes 802832 | tf_op jit(solution)/shard_map/psum | solution.py:119
  574.0 19.9 %all-reduce.3 = (bf16[1,2,512]{2,1,0:T(2,128)(2,1)S(1)}, bf16[1,2,512]{2,1,0:T(2,128)(2,1)S(1)}, bf16[1,2,128]{2,1,0:T(2,128)(2,1)S(1)}, bf16[1,169,4]{1,2,0:T(4...) all-reduce(bf16[1,2,512]{2,1,0:T(2,128)(2,1)S(1)} %fusion.288, ...), channel_id=1, replica_groups=mesh['section'=2,'dp'=4,'tensor'=4] {'dp'}, use_global_device_ids=true, to_apply=%region_63.64 | all-reduce | flops 4516 | bytes 18064 | tf_op jit(solution)/shard_map/psum | solution.py:79
  599.5 2.8 maximum_bitcast_fusion.1
  605.7 36.7 %all-reduce.34.cloned.1.call-done = (bf16[1,3,512,128]{2,3,1,0:T(8,128)(2,1)}, bf16[1,128,512]{2,1,0:T(8,128)(2,1)}, bf16[1,512,512]{2,1,0:T(8,128)(2,1)}, bf16[1,512,512]{2,1,0:T(8,128)(2,1)}) async-done(((bf16[1,3,512,128]{2,3,1,0:T(8,128)(2,1)}, bf16[1,128,512]{2,1,0:T(8,128)(2,1)}, bf16[1,512,512]{2,1,0:T(8,128)(2,1)}, bf16[1,512,512]{2,1,0:T(8,128)(2,1)}), (bf16[1,3,512,128]{2,3,1,0:T(8,128)(2,1)}, ...) | async-done | bytes 1572880 | tf_op jit(solution)/shard_map/psum | solution.py:81
  (792 shorter events, 294.4 us)
Async XLA Ops:
  7.2 51.7 %copy-start = (bf16[1,512,512]{2,1,0:T(8,128)(2,1)S(1)}, bf16[1,512,512]{2,1,0:T(8,128)(2,1)}, u32[]{:S(2)}) copy-start(bf16[1,512,512]{2,1,0:T(8,128)(2,1)} %param.23) | copy-start | bytes 1572868
  7.3 48.5 %all-reduce.16.cloned.1.call-start = ((), (), s32[]{:S(2)}) async-start(), calls=%async_computation | async-start | bytes 917504 | tf_op jit(solution)/shard_map/psum | solution.py:112
  9.1 105.8 %copy-start.157 = (f32[1,1,512]{2,1,0:T(1,128)}, f32[1,1,512]{2,1,0:T(1,128)S(1)}, u32[]{:S(2)}) copy-start(f32[1,1,512]{2,1,0:T(1,128)S(1)} %get-tuple-element.206) | copy-start | bytes 6148
  9.2 152.6 %copy-start.159 = (f32[1,1,512]{2,1,0:T(1,128)}, f32[1,1,512]{2,1,0:T(1,128)S(1)}, u32[]{:S(2)}) copy-start(f32[1,1,512]{2,1,0:T(1,128)S(1)} %get-tuple-element.207) | copy-start | bytes 6148
  18.4 38.8 %copy-start.132 = (bf16[2,4,4,32,49]{4,3,2,1,0:T(8,128)(2,1)}, bf16[2,4,4,32,49]{4,3,2,1,0:T(8,128)(2,1)S(1)}, u32[]{:S(2)}) copy-start(bf16[2,4,4,32,49]{4,3,2,1,0:T(8,128)(2,1)S(1)} %convolution_convert_fusion.14) | copy-start | bytes 301060
  19.9 78.0 %all-reduce.18.cloned.1.call-start = ((), (), s32[]{:S(2)}) async-start(), calls=%async_computation.1 | async-start | bytes 917504 | tf_op jit(solution)/shard_map/psum | solution.py:119
  20.3 77.6 %copy-start.161 = (f32[1,1,512]{2,1,0:T(1,128)}, f32[1,1,512]{2,1,0:T(1,128)S(1)}, u32[]{:S(2)}) copy-start(f32[1,1,512]{2,1,0:T(1,128)S(1)} %get-tuple-element.202) | copy-start | bytes 6148
  64.7 92.8 %all-reduce.20.cloned.1.call-start = ((), (), s32[]{:S(2)}) async-start(), calls=%async_computation.2 | async-start | bytes 917504 | tf_op jit(solution)/shard_map/psum | solution.py:112
  101.2 10.8 %collective-permute-start = (bf16[2,196,512]{2,0,1:T(2,128)(2,1)S(1)}, bf16[2,196,512]{2,0,1:T(2,128)(2,1)S(1)}, u32[]{:S(2)}, u32[]{:S(2)}) collective-permute-start(bf16[2,196,512]{2,0,1:T(2,128)(2,1)S(1)} %fusion.186), channel_id=1, source_target_pairs={{0,16},{1,17},{2,18},{3,19},{4,20},{5,21},{6,22},{7,23},{8,24},{9,... | collective-permute-start | bytes 1204232 | tf_op jit(solution)/shard_map/ppermute | solution.py:24
  122.7 84.6 %all-reduce.32.cloned.1.call-start = ((), (), s32[]{:S(2)}) async-start(), calls=%async_computation.8 | async-start | bytes 1835008 | tf_op jit(solution)/shard_map/psum | solution.py:141
  171.8 137.4 %all-reduce.30.cloned.1.call-start = ((), (), s32[]{:S(2)}) async-start(), calls=%async_computation.7 | async-start | bytes 1835008 | tf_op jit(solution)/shard_map/psum | solution.py:196
  214.3 11.5 %collective-permute-start.1 = (bf16[2,196,512]{2,0,1:T(2,128)(2,1)}, bf16[2,196,512]{2,0,1:T(2,128)(2,1)}, u32[]{:S(2)}, u32[]{:S(2)}) collective-permute-start(bf16[2,196,512]{2,0,1:T(2,128)(2,1)} %get-tuple-element.142), channel_id=1, source_target_pairs={{0,16},{1,17},{2,18},{3,19},{4,20},{5,21},{6,22},{7,23},{8,24},{9,... | collective-permute-start | bytes 1204232 | tf_op jit(solution)/shard_map/ppermute | solution.py:24
  254.9 13.1 %copy-start.58 = (bf16[1,2,4,49,128]{3,4,2,1,0:T(8,128)(2,1)}, bf16[1,2,4,49,128]{3,4,2,1,0:T(8,128)(2,1)S(1)}, u32[]{:S(2)}) copy-start(bf16[1,2,4,49,128]{3,4,2,1,0:T(8,128)(2,1)S(1)} %copy.389) | copy-start | bytes 301060
  267.7 110.8 %all-reduce.22.cloned.1.call-start = ((), (), s32[]{:S(2)}) async-start(), calls=%async_computation.3 | async-start | bytes 917504 | tf_op jit(solution)/shard_map/psum | solution.py:141
  279.6 27.1 %copy-start.148 = (f32[2,2,8,49]{3,2,1,0:T(8,128)S(1)}, f32[2,2,8,49]{3,2,1,0:T(8,128)}, u32[]{:S(2)}) copy-start(f32[2,2,8,49]{3,2,1,0:T(8,128)} %get-tuple-element.237) | copy-start | bytes 18820
  319.2 11.6 %collective-permute-start.2 = (bf16[2,196,512]{2,0,1:T(2,128)(2,1)S(1)}, bf16[2,196,512]{2,0,1:T(2,128)(2,1)S(1)}, u32[]{:S(2)}, u32[]{:S(2)}) collective-permute-start(bf16[2,196,512]{2,0,1:T(2,128)(2,1)S(1)} %fusion.263), channel_id=1, source_target_pairs={{16,0},{17,1},{18,2},{19,3},{20,4},{21,5},{22,6},{23,7},{24,8},{25... | collective-permute-start | bytes 1204232 | tf_op jit(solution)/shard_map/ppermute | solution.py:24
  321.7 13.0 %copy-start.106 = (f32[2,4,49,512]{3,2,1,0:T(8,128)}, f32[2,4,49,512]{3,2,1,0:T(8,128)S(1)}, u32[]{:S(2)}) copy-start(f32[2,4,49,512]{3,2,1,0:T(8,128)S(1)} %get-tuple-element.221) | copy-start | bytes 2408452
  344.8 94.6 %all-reduce.24.cloned.1.call-start = ((), (), s32[]{:S(2)}) async-start(), calls=%async_computation.4 | async-start | bytes 917504 | tf_op jit(solution)/shard_map/psum | solution.py:196
  406.3 98.7 %all-reduce.26.cloned.1.call-start = ((), (), s32[]{:S(2)}) async-start(), calls=%async_computation.5 | async-start | bytes 917504 | tf_op jit(solution)/shard_map/psum | solution.py:141
  447.6 11.4 %collective-permute-start.3 = (bf16[2,196,512]{2,0,1:T(2,128)(2,1)S(1)}, bf16[2,196,512]{2,0,1:T(2,128)(2,1)S(1)}, u32[]{:S(2)}, u32[]{:S(2)}) collective-permute-start(bf16[2,196,512]{2,0,1:T(2,128)(2,1)S(1)} %convert_element_type.483), channel_id=1, source_target_pairs={{16,0},{17,1},{18,2},{19,3},{20,4},{21,5},{22,6},{23,7},{24,8},{25... | collective-permute-start | bytes 1204232 | tf_op jit(solution)/shard_map/ppermute | solution.py:24
  471.6 96.3 %all-reduce.28.cloned.1.call-start = ((), (), s32[]{:S(2)}) async-start(), calls=%async_computation.6 | async-start | bytes 1835008 | tf_op jit(solution)/shard_map/psum | solution.py:119
  532.4 110.1 %all-reduce.34.cloned.1.call-start = ((), (), s32[]{:S(2)}) async-start(), calls=%async_computation.9 | async-start | bytes 3145728 | tf_op jit(solution)/shard_map/psum | solution.py:81
  539.6 28.3 %copy-start.162 = (f32[1,1,512]{2,1,0:T(1,128)S(1)}, f32[1,1,512]{2,1,0:T(1,128)}, u32[]{:S(2)}) copy-start(f32[1,1,512]{2,1,0:T(1,128)} %copy-done.161) | copy-start | bytes 6148
  573.2 24.1 %copy-start.89 = (bf16[2,11,14,512]{3,0,2,1:T(2,128)(2,1)S(1)}, bf16[2,11,14,512]{3,0,2,1:T(2,128)(2,1)}, u32[]{:S(2)}) copy-start(bf16[2,11,14,512]{3,0,2,1:T(2,128)(2,1)} %slice.418) | copy-start | bytes 946180
  (215 other events, 531.9 us)
Sparse Core Ops, SparseCore 0:
  20.0 35.7 all-reduce.15
  64.8 33.0 all-reduce.17
  122.8 34.6 all-reduce.19
  171.9 35.3 all-reduce.31
  267.8 37.3 all-reduce.29
  345.0 33.4 all-reduce.21
  406.4 32.9 all-reduce.23
  471.7 33.2 all-reduce.25
  532.5 35.3 all-reduce.27
  571.5 70.8 all-reduce.33
where the time goes:
time: 668 us; the launch traced here: 656 us
  waiting for transfers between devices  289 us (43%)
  local copies, waits for them, and re-layouts  125 us (19%)
  other arithmetic  108 us (16%)
  matrix products  83.1 us (12%)
  blocking collectives  19.9 us (3%)
  between operations  17.6 us (3%)
  starting transfers between devices  12.9 us (2%)
    psum x3, waiting for transfers between devices, block_backward(): lax.psum(partial_second.astype(jnp.bfloat16), 'tensor').astype(jnp.float32)  74.4 us
    psum x2, waiting for transfers between devices, block_forward(): lax.psum(part_sum.astype(jnp.bfloat16), 'tensor').astype(jnp.float32)  66.4 us
    psum x2, waiting for transfers between devices, block_forward(): lax.psum(part_second.astype(jnp.bfloat16), 'tensor').astype(jnp.float32)  60.6 us
    psum x1, waiting for transfers between devices, data_sum(): lax.psum(grads[2].astype(jnp.bfloat16), 'dp').astype(jnp.float32)  36.7 us
    psum x2, waiting for transfers between devices, block_backward(): lax.psum(partial_first.astype(jnp.bfloat16), 'tensor').astype(jnp.float32)  30.8 us
    unnamed x451, local copies, waits for them, and re-layouts  20.4 us
    ppermute x4, waiting for transfers between devices, from_behind(): return lax.ppermute(array, axis, pairs)  20.3 us
    psum x1, blocking collectives, data_sum(): lax.psum(grads[0].astype(jnp.bfloat16), 'dp').astype(jnp.float32)  19.9 us
  transfers between devices with their start and end apart: 14, of which 13 were waited for; matrix products, arithmetic and copies ran while one was open for 16% of the time, Pallas kernels for 0%

commit v1 on v0

v1 whole, which is shorter than its diff:
```python
import functools

import jax
import jax.numpy as jnp
import numpy as np
from jax import lax
from jax.experimental import pallas as pl
from jax.experimental.pallas import tpu as pltpu
from jax.sharding import PartitionSpec as P

D = 512
HEAD_DIM = 32
WIN = 7
SIDE = 14
SHIFT = 3
PIX = 196
WTOK = 49
REL = 169
NWIN = 4

ROWS = 64
M = NWIN * ROWS
TOK = 208
GROUP = 4
LANES = GROUP * HEAD_DIM
WIDE = GROUP * ROWS
SLOTS = 4

EPS = 1e-05
SCALE = HEAD_DIM ** (-0.5)
BF = jnp.bfloat16
F32 = jnp.float32
HIGHEST = lax.Precision.HIGHEST

SEC, DP, TEN = "section", "dp", "tensor"

(
    X,
    NORMED,
    XHAT1,
    R1,
    CTX,
    MIDDLE,
    NORMED2,
    XHAT2,
    R2,
    HIDDEN,
    Y,
    GMLP,
    GPRE,
    GMIDDLE,
    GBRANCH,
    SUMS_B,
    GQKV,
    DOWN,
    SUMS_A,
    SCORESUM,
    PV,
    PERM,
    PERM_T,
    BIAS,
    REGION,
    FC1W,
    FC2W,
    PROBS,
    PROJW,
    QKV,
    QKVW,
    SLOPE,
) = range(32)


def dot(a, b, ca, cb):
    return lax.dot_general(a, b, (((ca,), (cb,)), ((), ())), preferred_element_type=F32)


class Env:
    def __init__(self, refs, copies_in, copies_out):
        self.refs, self.copies_in, self.copies_out = refs, dict(copies_in), dict(copies_out)
        self.started = []

    def __getitem__(self, name):
        return self.refs[name]

    def need(self, name):
        copy = self.copies_in.pop(name, None)
        if copy is not None:
            copy.wait()
        return self.refs[name]

    def emit(self, name):
        copy = self.copies_out.pop(name, None)
        if copy is not None:
            copy.start()
            self.started.append(copy)

    def finish(self):
        for name in list(self.copies_in):
            self.need(name)
        for name in list(self.copies_out):
            self.emit(name)
        for copy in self.started:
            copy.wait()


def head_masks():
    lane = lax.broadcasted_iota(jnp.int32, (1, LANES), 1) // HEAD_DIM
    return [(lane == h).astype(F32) for h in range(GROUP)]


def spread(rows, masks):
    return jnp.concatenate([rows * mask.astype(BF) for mask in masks], axis=0)


def gather_heads(stacked, masks):
    total = stacked[0:ROWS] * masks[0]
    for h in range(1, GROUP):
        total = total + stacked[h * ROWS : (h + 1) * ROWS] * masks[h]
    return total


def norm_of(values):
    center = values - jnp.mean(values, -1, keepdims=True)
    r = lax.rsqrt(jnp.mean(center * center, -1, keepdims=True) + EPS)
    return center * r, r


def joined_qkv(ref):
    return jnp.concatenate([ref[0], ref[1], ref[2]], axis=1)


def forward_attention(env):
    masks = head_masks()
    tiles = dot(env[PERM][...], env.need(X)[...], 1, 0)
    xhat, r = norm_of(tiles)
    env[XHAT1][...] = xhat
    env[R1][...] = jnp.broadcast_to(r, (M, 128))
    env.emit(XHAT1)
    env.emit(R1)
    normed = (xhat * env[PV][0:1, :] + env[PV][2:3, :]).astype(BF)
    env[NORMED][...] = normed
    env.emit(NORMED)
    branch = jnp.zeros((M, D), F32)
    for j in range(SLOTS):
        weight = joined_qkv(env.need((QKVW, j)))
        packed = (dot(normed, weight, 1, 0) + env[PV][12 + j : 13 + j, 0 : 3 * LANES]).astype(BF)
        env[(QKV, j)][...] = packed
        env.emit((QKV, j))
        parts = []
        for w in range(NWIN):
            rows = slice(w * ROWS, (w + 1) * ROWS)
            q = packed[rows, 0:LANES]
            k = packed[rows, LANES : 2 * LANES]
            v = packed[rows, 2 * LANES : 3 * LANES]
            scores = dot(k, spread(q, masks), 1, 1) * SCALE + env[BIAS][j] + env[REGION][w]
            exps = jnp.exp(scores - jnp.max(scores, 0, keepdims=True))
            probs = exps / jnp.sum(exps, 0, keepdims=True)
            env[(PROBS, j)][w] = probs
            parts.append(gather_heads(dot(probs.astype(BF), v, 0, 0), masks))
        env.emit((PROBS, j))
        context = jnp.concatenate(parts, axis=0).astype(BF)
        env[CTX][j] = context
        branch = branch + dot(context, env.need((PROJW, j))[...], 1, 0)
    env.emit(CTX)
    env[MIDDLE][...] = tiles + branch + env[PV][4:5, :]
    env.emit(MIDDLE)


def forward_mlp(env):
    middle = env.need(MIDDLE)[...]
    xhat, r = norm_of(middle)
    env[XHAT2][...] = xhat
    env[R2][...] = jnp.broadcast_to(r, (M, 128))
    env.emit(XHAT2)
    env.emit(R2)
    normed = (xhat * env[PV][1:2, :] + env[PV][3:4, :]).astype(BF)
    env[NORMED2][...] = normed
    env.emit(NORMED2)
    total = middle + env[PV][5:6, :]
    for j in range(SLOTS):
        pre = dot(normed, env.need((FC1W, j))[...], 1, 0) + env[PV][8 + j : 9 + j, :]
        phi = 0.5 * (1.0 + lax.erf(pre * (0.5**0.5)))
        hidden = (pre * phi).astype(BF)
        env[(SLOPE, j)][...] = phi + pre * jnp.exp(-0.5 * pre * pre) * (2.0 * np.pi) ** -0.5
        env.emit((SLOPE, j))
        env[HIDDEN][j] = hidden
        total = total + dot(hidden, env.need((FC2W, j))[...], 1, 0)
    env[Y][...] = dot(env[PERM_T][...], total.astype(BF), 1, 0).astype(BF)
    env.emit(Y)
    env.emit(HIDDEN)


def backward_norm(grad, xhat, r, gain):
    u = grad * gain
    return r * (u - jnp.mean(u, -1, keepdims=True) - xhat * jnp.mean(u * xhat, -1, keepdims=True))


def column_sum(values):
    return jnp.sum(values, 0, keepdims=True)


def backward_mlp(env):
    gmlp = env.need(GMLP)[...]
    gtiles = gmlp.astype(F32)
    sums = env[SUMS_B]
    sums[3:4, :] = column_sum(gtiles)
    total = jnp.zeros((M, D), F32)
    for j in range(SLOTS):
        gact = dot(gmlp, env.need((FC2W, j))[...], 1, 1)
        gpre = (gact * env.need((SLOPE, j))[...]).astype(BF)
        env[GPRE][j] = gpre
        sums[4 + j : 5 + j, :] = column_sum(gpre.astype(F32))
        total = total + dot(gpre, env.need((FC1W, j))[...], 1, 1)
    env.emit(GPRE)
    xhat = env.need(XHAT2)[...]
    r = env.need(R2)[:, 0:1]
    sums[0:1, :] = column_sum(total * xhat)
    sums[1:2, :] = column_sum(total)
    gmiddle = gtiles + backward_norm(total, xhat, r, env[PV][1:2, :])
    env[GMIDDLE][...] = gmiddle
    env.emit(GMIDDLE)
    gbranch = gmiddle.astype(BF)
    env[GBRANCH][...] = gbranch
    env.emit(GBRANCH)
    sums[2:3, :] = column_sum(gbranch.astype(F32))
    env.emit(SUMS_B)


def backward_attention(env):
    masks = head_masks()
    sums = env[SUMS_A]
    sums[...] = jnp.zeros_like(sums)
    gbranch = env.need(GBRANCH)[...]
    total = jnp.zeros((M, D), F32)
    for j in range(SLOTS):
        gcontext = dot(gbranch, env.need((PROJW, j))[...], 1, 1).astype(BF)
        packed = env.need((QKV, j))[...]
        env.need((PROBS, j))
        score_sum = None
        parts = []
        for w in range(NWIN):
            rows = slice(w * ROWS, (w + 1) * ROWS)
            q = spread(packed[rows, 0:LANES], masks)
            k = packed[rows, LANES : 2 * LANES]
            v = packed[rows, 2 * LANES : 3 * LANES]
            up = spread(gcontext[rows], masks)
            probs = env[(PROBS, j)][w]
            gprobs = dot(v, up, 1, 1)
            gscores = probs * (gprobs - jnp.sum(gprobs * probs, 0, keepdims=True))
            low = gscores.astype(BF)
            wide = low.astype(F32)
            score_sum = wide if score_sum is None else score_sum + wide
            gv = dot(probs.astype(BF), up, 1, 0)
            gk = dot(low, q, 1, 0) * SCALE
            gq = gather_heads(dot(low, k, 0, 0), masks) * SCALE
            parts.append(jnp.concatenate([gq, gk, gv], axis=1).astype(BF))
        env[SCORESUM][j] = score_sum
        grads = jnp.concatenate(parts, axis=0)
        env[GQKV][j] = grads
        sums[4 + j : 5 + j, 0 : 3 * LANES] = column_sum(grads.astype(F32))
        total = total + dot(grads, joined_qkv(env.need((QKVW, j))), 1, 1)
    env.emit(SCORESUM)
    env.emit(GQKV)
    xhat = env.need(XHAT1)[...]
    r = env.need(R1)[:, 0:1]
    sums[0:1, :] = column_sum(total * xhat)
    sums[1:2, :] = column_sum(total)
    env.emit(SUMS_A)
    down = env.need(GMIDDLE)[...] + backward_norm(total, xhat, r, env[PV][0:1, :])
    env[DOWN][...] = dot(env[PERM_T][...], down.astype(BF), 1, 0).astype(BF)
    env.emit(DOWN)


def shapes_of():
    table = {
        X: ((TOK, D), BF),
        NORMED: ((M, D), BF),
        XHAT1: ((M, D), F32),
        R1: ((M, 128), F32),
        CTX: ((SLOTS, M, LANES), BF),
        MIDDLE: ((M, D), F32),
        NORMED2: ((M, D), BF),
        XHAT2: ((M, D), F32),
        R2: ((M, 128), F32),
        HIDDEN: ((SLOTS, M, D), BF),
        Y: ((TOK, D), BF),
        GMLP: ((M, D), BF),
        GPRE: ((SLOTS, M, D), BF),
        GMIDDLE: ((M, D), F32),
        GBRANCH: ((M, D), BF),
        SUMS_B: ((8, D), F32),
        GQKV: ((SLOTS, M, 3 * LANES), BF),
        DOWN: ((TOK, D), BF),
        SUMS_A: ((8, D), F32),
        SCORESUM: ((SLOTS, ROWS, WIDE), F32),
    }
    for j in range(SLOTS):
        table[(QKVW, j)] = ((3, D, LANES), BF)
        table[(PROJW, j)] = ((LANES, D), BF)
        table[(FC1W, j)] = ((D, D), BF)
        table[(FC2W, j)] = ((D, D), BF)
        table[(QKV, j)] = ((M, 3 * LANES), BF)
        table[(PROBS, j)] = ((NWIN, ROWS, WIDE), F32)
        table[(SLOPE, j)] = ((M, D), F32)
    return table


SHAPES = shapes_of()


def per_slot(*names):
    return [(name, j) for j in range(SLOTS) for name in names]


ATT_WEIGHTS = per_slot(QKVW, PROJW)
MLP_WEIGHTS = per_slot(FC1W, FC2W)
ATT_OUT = [XHAT1, R1, NORMED] + per_slot(QKV, PROBS) + [CTX, MIDDLE]
MLP_OUT = [XHAT2, R2, NORMED2] + per_slot(SLOPE) + [Y, HIDDEN]
BACK_MLP_OUT = [GPRE, GMIDDLE, GBRANCH, SUMS_B]
BACK_ATT_OUT = [SCORESUM, GQKV, SUMS_A, DOWN]


def run_stages(stages, active, section, small, arrays, ins, outs, keep=(), scratch=()):
    small_names = list(small)
    kept = [name for name in outs if name in keep]
    n_small, n_in, n_kept, n_out = len(small_names), len(ins), len(kept), len(outs)
    local = [name for name in list(ins) + list(outs) + list(scratch)]

    def kernel(*refs):
        place = refs[0]
        at = 1
        env_refs = dict(zip(small_names, refs[at : at + n_small]))
        at += n_small
        in_hbm = refs[at : at + n_in]
        at += n_in + n_kept
        out_hbm = refs[at : at + n_out]
        at += n_out
        env_refs.update(zip(local, refs[at : at + len(local)]))
        sems = refs[at + len(local)]

        @pl.when(place[0] == active)
        def _():
            copies_in = {}
            for i, name in enumerate(ins):
                copies_in[name] = pltpu.make_async_copy(in_hbm[i], env_refs[name], sems.at[i])
                copies_in[name].start()
            copies_out = {
                name: pltpu.make_async_copy(env_refs[name], out_hbm[i], sems.at[n_in + i])
                for i, name in enumerate(outs)
            }
            env = Env(env_refs, copies_in, copies_out)
            for stage in stages:
                stage(env)
            env.finish()

    vmem = pl.BlockSpec(memory_space=pltpu.VMEM)
    hbm = pl.BlockSpec(memory_space=pl.ANY)
    results = pl.pallas_call(
        kernel,
        out_shape=[jax.ShapeDtypeStruct(*SHAPES[name]) for name in outs],
        in_specs=[pl.BlockSpec(memory_space=pltpu.SMEM)]
        + [vmem] * n_small
        + [hbm] * (n_in + n_kept),
        out_specs=[hbm] * n_out,
        scratch_shapes=[pltpu.VMEM(*SHAPES[name]) for name in local]
        + [pltpu.SemaphoreType.DMA((n_in + n_out,))],
        input_output_aliases={
            1 + n_small + n_in + i: outs.index(name) for i, name in enumerate(kept)
        },
        compiler_params=pltpu.CompilerParams(vmem_limit_bytes=48 * 1024 * 1024),
        cost_estimate=pl.CostEstimate(
            flops=5_000_000_000, bytes_accessed=8_000_000, transcendentals=1_000_000
        ),
    )(
        section,
        *[small[name] for name in small_names],
        *[arrays[name] for name in ins],
        *[arrays[name] for name in kept],
    )
    arrays.update(zip(outs, results))


def tile_places(shift):
    places = np.full((NWIN, ROWS), -1, np.int32)
    for w in range(NWIN):
        for r in range(WTOK):
            i = (w // 2) * WIN + r // WIN
            j = (w % 2) * WIN + r % WIN
            places[w, r] = ((i + shift) % SIDE) * SIDE + (j + shift) % SIDE
    return places.reshape(M)


def permutations(shifted):
    places = jnp.where(shifted, jnp.asarray(tile_places(SHIFT)), jnp.asarray(tile_places(0)))
    tokens = jnp.arange(TOK, dtype=jnp.int32)
    forth = (places[:, None] == tokens[None, :]).astype(BF)
    back = (tokens[:, None] == places[None, :]).astype(BF)
    return forth, back


def region_bias(regions, shifted):
    stripes = SIDE // WIN
    tiled = (
        regions.reshape(stripes, WIN, stripes, WIN)
        .transpose(0, 2, 1, 3)
        .reshape(stripes * stripes, WIN * WIN)
    )
    tiled = jnp.pad(tiled, ((0, 0), (0, ROWS - WTOK)))
    differ = (tiled[:, :, None] != tiled[:, None, :]) & shifted
    return jnp.tile(jnp.where(differ, -100.0, 0.0).astype(F32), (1, 1, GROUP))


def xor_permute(array, by):
    devices = lax.axis_size(TEN)
    return lax.ppermute(array, TEN, [(i, i ^ by) for i in range(devices)])


def gather_slots(array):
    across = xor_permute(array, 2)
    return [array, xor_permute(array, 1), across, xor_permute(across, 1)]


def section_permute(array, source):
    return lax.ppermute(array, SEC, [(source, 1 - source)])


def line_sum(part):
    devices = lax.axis_size(DP)
    if devices != 4:
        return lax.psum(part, DP)
    inner = lax.axis_index(DP)
    inner = (inner == 1) | (inner == 2)
    part = part + lax.ppermute(part, DP, [(0, 1), (3, 2)])
    part = part + lax.ppermute(part, DP, [(1, 2), (2, 1)])
    return jnp.where(inner, part, lax.ppermute(part, DP, [(1, 0), (2, 3)]))


def slot_sum(parts):
    near = xor_permute(jnp.stack([parts[1].astype(BF), parts[3].astype(BF)]), 1)
    far = (parts[2] + near[1].astype(F32)).astype(BF)
    far = xor_permute(far, 2)
    return (parts[0] + near[0].astype(F32) + far.astype(F32)).astype(BF)


def local(
    images,
    out_grad,
    ln_gain,
    ln_bias,
    qkv_weight,
    qv_bias,
    pos_table,
    proj_weight,
    out_bias,
    fc1_weight,
    fc1_bias,
    fc2_weight,
    rel_index,
    regions,
):
    section_id = lax.axis_index(SEC)
    shifted = section_id == 1
    section = section_id.astype(jnp.int32).reshape(1)
    tensor = lax.axis_index(TEN)

    pad = jnp.zeros((LANES,), F32)
    row = jnp.concatenate([qv_bias[0, 0], pad, qv_bias[0, 1], pad])
    table = jnp.pad(pos_table[0].reshape(-1), (0, 2 * D - REL * GROUP)).reshape(2, D)
    own_small = jnp.concatenate([fc1_bias[0][None], row[None], table], axis=0)
    small_slots = gather_slots(own_small)
    arrays = {}
    for name, own in (
        (QKVW, qkv_weight[0]),
        (PROJW, proj_weight[0]),
        (FC1W, fc1_weight[0]),
        (FC2W, fc2_weight[0]),
    ):
        for j, part in enumerate(gather_slots(own)):
            arrays[name, j] = part

    forth, back = permutations(shifted)
    rel = jnp.pad(rel_index, ((0, ROWS - WTOK), (0, ROWS - WTOK)), constant_values=-1)
    onehot = (rel.T[None] == jnp.arange(REL, dtype=jnp.int32)[:, None, None]).astype(F32)
    heads = jnp.stack([part[2:4].reshape(-1)[: REL * GROUP] for part in small_slots])
    heads = heads.reshape(SLOTS, REL, GROUP)
    bias = jnp.einsum("jrh,rca->jcha", heads, onehot, precision=HIGHEST)
    bias = bias.reshape(SLOTS, ROWS, WIDE)
    bias = jnp.where(jnp.arange(ROWS)[None, :, None] < WTOK, bias, -1e30)
    region = region_bias(regions, shifted)
    vectors = jnp.concatenate(
        [ln_gain[0], ln_bias[0], out_bias[0], jnp.zeros((2, D), F32)]
        + [part[0:1] for part in small_slots]
        + [part[1:2] for part in small_slots],
        axis=0,
    )
    all_small = {PV: vectors, PERM: forth, PERM_T: back, BIAS: bias, REGION: region}

    def small(*names):
        return {name: all_small[name] for name in names}

    images_each = images.shape[0] // lax.axis_size(TEN)

    def own_image(batch):
        one = lax.dynamic_slice_in_dim(batch, tensor * images_each, images_each, 0)
        return jnp.pad(one.reshape(PIX, D), ((0, TOK - PIX), (0, 0)))

    arrays[X] = own_image(images)
    run_stages(
        [forward_attention], 0, section, small(PV, PERM, BIAS, REGION),
        arrays, [X] + ATT_WEIGHTS, ATT_OUT,
    )
    run_stages(
        [forward_mlp], 0, section, small(PV, PERM_T),
        arrays, [MIDDLE] + MLP_WEIGHTS, MLP_OUT,
    )
    upstream = own_image(out_grad)
    arrays[X] = section_permute(arrays[Y], 0)
    arrays[GMLP] = dot(forth, upstream, 1, 0).astype(BF)
    outs = [NORMED, CTX, NORMED2, Y, HIDDEN, GPRE, GBRANCH, SUMS_B] + BACK_ATT_OUT
    saved = dict(arrays)
    run_stages(
        [forward_attention, forward_mlp, backward_mlp, backward_attention], 1, section,
        small(PV, PERM, PERM_T, BIAS, REGION),
        arrays, [X] + ATT_WEIGHTS + MLP_WEIGHTS + [GMLP], outs,
        keep=(NORMED, CTX, NORMED2, Y, HIDDEN),
        scratch=[XHAT1, R1, MIDDLE, XHAT2, R2, GMIDDLE]
        + per_slot(QKV, PROBS, SLOPE),
    )
    arrived = section_permute(arrays[DOWN], 1)
    gmlp = dot(forth, jnp.where(shifted, upstream, arrived), 1, 0).astype(BF)
    arrays[GMLP] = gmlp
    hidden = arrays[HIDDEN]
    fc2_parts = [dot(hidden[j], gmlp, 0, 0) for j in range(SLOTS)]
    fc2_grad = line_sum(slot_sum(fc2_parts))
    run_stages(
        [backward_mlp], 0, section, small(PV),
        arrays, [GMLP] + MLP_WEIGHTS + per_slot(SLOPE) + [XHAT2, R2], BACK_MLP_OUT,
        keep=(GPRE, GBRANCH, SUMS_B),
    )
    fc1_parts = [dot(arrays[NORMED2], arrays[GPRE][j], 0, 0) for j in range(SLOTS)]
    fc1_grad = line_sum(slot_sum(fc1_parts))
    run_stages(
        [backward_attention], 0, section, small(PV, PERM_T),
        arrays,
        [GBRANCH] + ATT_WEIGHTS + per_slot(QKV, PROBS) + [XHAT1, R1, GMIDDLE],
        BACK_ATT_OUT, keep=BACK_ATT_OUT,
    )
    sums_a, sums_b = arrays[SUMS_A], arrays[SUMS_B]
    scores = arrays[SCORESUM].reshape(SLOTS, ROWS, GROUP, ROWS)
    table_grad = jnp.einsum("jcha,rca->jrh", scores, onehot, precision=HIGHEST)
    table_grad = jnp.pad(table_grad.reshape(SLOTS, -1), ((0, 0), (0, 2 * D - REL * GROUP)))
    table_grad = table_grad.reshape(SLOTS, 2, D)
    shared = jnp.concatenate([sums_a[0:1], sums_b[0:1], sums_a[1:2], sums_b[1:2], sums_b[2:4]])
    tail_parts = []
    for j in range(SLOTS):
        qkv_part = dot(arrays[NORMED], arrays[GQKV][j], 0, 0)
        proj_part = dot(arrays[CTX][j], arrays[GBRANCH], 0, 0)
        rows = jnp.concatenate(
            [proj_part, shared, sums_b[4 + j : 5 + j], sums_a[4 + j : 5 + j], table_grad[j]]
            + [jnp.zeros((6, D), F32)]
        )
        tail_parts.append((qkv_part, rows))
    qkv_grad = line_sum(slot_sum([part[0] for part in tail_parts]))
    rest = line_sum(slot_sum([part[1] for part in tail_parts]))

    def spread_images(own):
        mine, near, far, both = gather_slots(own[:PIX])
        parts = jnp.stack([mine, near, far, both])
        order = jnp.arange(SLOTS) ^ tensor
        return parts[order]

    section_out = spread_images(arrays[Y])
    input_grad = spread_images(arrays[DOWN]).astype(F32)
    qkv_grad = qkv_grad.astype(F32)
    rest = rest.astype(F32)
    head = rest[LANES:]
    outs = (
        section_out,
        input_grad,
        head[0:2],
        head[2:4],
        jnp.stack([qkv_grad[:, i * LANES : (i + 1) * LANES] for i in range(3)]),
        jnp.stack([head[7, 0:LANES], head[7, 2 * LANES : 3 * LANES]]),
        head[8:10].reshape(-1)[: REL * GROUP].reshape(REL, GROUP),
        rest[:LANES],
        head[4:6],
        fc1_grad.astype(F32),
        head[6],
        fc2_grad.astype(F32),
    )
    return tuple(out[None] for out in outs)


def solution(mesh):
    placed = (
        P(DP, None, None),
        P(DP, None, None),
        P(SEC, None, None),
        P(SEC, None, None),
        P(SEC, None, None, TEN),
        P(SEC, None, TEN),
        P(SEC, None, TEN),
        P(SEC, TEN, None),
        P(SEC, None, None),
        P(SEC, None, TEN),
        P(SEC, TEN),
        P(SEC, TEN, None),
        P(),
        P(),
    )
    return jax.shard_map(
        local,
        mesh=mesh,
        in_specs=placed,
        out_specs=(
            P(SEC, DP, None, None),
            P(SEC, DP, None, None),
            P(SEC, None, None),
            P(SEC, None, None),
            P(SEC, None, None, TEN),
            P(SEC, None, TEN),
            P(SEC, None, TEN),
            P(SEC, TEN, None),
            P(SEC, None, None),
            P(SEC, None, TEN),
            P(SEC, TEN),
            P(SEC, TEN, None),
        ),
        check_vma=False,
    )
```

time: 668 us -> 274 us (0.41); the launches traced: 656 us -> 269 us
  waiting for transfers between devices: 289 us -> 88.7 us
  local copies, waits for them, and re-layouts: 125 us -> 39.2 us
  other arithmetic: 108 us -> 24.7 us
  matrix products: 83.1 us -> 30.3 us
  Pallas kernels: 0 us -> 36.9 us
  starting transfers between devices: 12.9 us -> 47.6 us
  blocking collectives: 19.9 us -> 0 us
  between operations: 17.6 us -> 1.92 us
    psum x10 -> x0, waiting for transfers between devices: 269 us -> none  [the longest x3 74.4 us: block_backward(): lax.psum(partial_second.astype(jnp.bfloat16), 'tensor').astype(jnp.float32)]
    ppermute x4 -> x43, waiting for transfers between devices: 20.3 us -> 88.7 us  [the longest x29 31.6 us: xor_permute(): return lax.ppermute(array, TEN, [(i, i ^ by) for i in range(devices)])]
    reduce_sum x41 -> x0, other arithmetic: 56 us -> none  [the longest x8 14.7 us: layer_norm(): center = values - jnp.mean(values, -1, keepdims=True)]
    dot_general x61 -> x20, matrix products: 83.1 us -> 30.3 us  [the longest x18 22 us: dot(): lax.dot_general(a, b, (((ca,), (cb,)), ((), ())), preferred_element_type=...]
    pallas_call x0 -> x5, Pallas kernels: none -> 36.9 us  [run_stages(): pl.pallas_call(kernel, out_shape=[jax.ShapeDtypeStruct(*SHAPES[name]) for...]
    ppermute x4 -> x43, starting transfers between devices: 11.3 us -> 47.6 us  [the longest x4 19.8 us: line_sum(): part = part + lax.ppermute(part, DP, [(0, 1), (3, 2)])]
    slice x52 -> x11, local copies, waits for them, and re-layouts: 24.3 us -> 0.68 us  [the longest x1 0.58 us: local(): head[6]]
    psum x1 -> x0, blocking collectives: 19.9 us -> none  [data_sum(): lax.psum(grads[0].astype(jnp.bfloat16), 'dp').astype(jnp.float32)]
  transfers between devices with their start and end apart: 14 -> 43, of which waited for: 13 -> 14; matrix products, arithmetic and copies ran while one was open for 16% -> 31% of each run, Pallas kernels for 0% -> 12%
where the time goes in v1:
time: 274 us; the launch traced here: 269 us
  waiting for transfers between devices  88.7 us (32%)
  starting transfers between devices  47.6 us (17%)
  local copies, waits for them, and re-layouts  39.2 us (14%)
  Pallas kernels  36.9 us (13%)
  matrix products  30.3 us (11%)
  other arithmetic  24.7 us (9%)
    pallas_call x5, Pallas kernels, run_stages(): pl.pallas_call(kernel, out_shape=[jax.ShapeDtypeStruct(*SHAPES[name]) for...  36.9 us
    ppermute x29, waiting for transfers between devices, xor_permute(): return lax.ppermute(array, TEN, [(i, i ^ by) for i in range(devices)])  31.6 us
    ppermute x4, waiting for transfers between devices, line_sum(): return jnp.where(inner, part, lax.ppermute(part, DP, [(1, 0), (2, 3)]))  30.6 us
    dot_general x18, matrix products, dot(): lax.dot_general(a, b, (((ca,), (cb,)), ((), ())), preferred_element_type=...  22 us
    ppermute x2, waiting for transfers between devices, section_permute(): return lax.ppermute(array, SEC, [(source, 1 - source)])  21.9 us
    ppermute x4, starting transfers between devices, line_sum(): part = part + lax.ppermute(part, DP, [(0, 1), (3, 2)])  19.8 us
    ppermute x29, starting transfers between devices, xor_permute(): return lax.ppermute(array, TEN, [(i, i ^ by) for i in range(devices)])  16.2 us
    unnamed x95, local copies, waits for them, and re-layouts  14.6 us
  transfers between devices with their start and end apart: 43, of which 14 were waited for; matrix products, arithmetic and copies ran while one was open for 31% of the time, Pallas kernels for 12%

profile of v1, /device:TPU:0, one launch (start us, length us, event | category | flops | bytes accessed | tf_op | source)
XLA Modules:
  0.0 269.3 jit_solution(10615695547213775047)
XLA Ops:
  3.1 3.0 %collective-permute-start.1 = (f32[4,512]{1,0:T(4,128)S(1)}, f32[4,512]{1,0:T(4,128)S(1)}, u32[]{:S(2)}, u32[]{:S(2)}) collective-permute-start(f32[4,512]{1,0:T(4,128)S(1)} %pad_maximum_fusion.6), channel_id=1, source_target_pairs={{0,2},{1,3},{2,0},{3,1},{4,6},{5,7},{6,4},{7,5},{8,10},{9,11},{10,... | collective-permute-start | bytes 24584 | tf_op jit(solution)/shard_map/ppermute | solution.py:415
  12.7 2.3 constant_dynamic-slice_fusion
  22.6 5.7 %fusion.16 = f32[4,64,4,64]{3,2,0,1:T(4,128)} fusion(pred[169,64,64,1]{0,1,2,3:T(32,128)(4,1)} %fusion, f32[1,169,4]{1,2,0:T(4,128)S(1)} %copy.48, f32[1,169,4]{1,2,0:T(4,128)S(1)} %copy.47, f32[1,169,4]{1,2,0:T(4,128)S(1)} %copy.46, f32[1,169,4]{1,2,0:T(4,128)S(1)} %copy-done.37), kind=kOutput, calls=%fused_computation.31 | convolution fusion | flops 132915120 | bytes 965184 | tf_op jit(solution)/shard_map/jrh,rca->jcha/dot_general | solution.py:486
  33.9 10.3 %collective-permute-done.12.refs_9_.refs_20_.refs_8_ = bf16[512,512]{1,0:T(8,128)(2,1)} collective-permute-done((bf16[512,512]{1,0:T(8,128)(2,1)S(1)}, bf16[512,512]{1,0:T(8,128)(2,1)}, u32[]{:S(2)}, u32[]{:S(2)}) %collective-permute-start.12) | collective-permute-done | bytes 524320 | tf_op jit(solution)/shard_map/ppermute | solution.py:415
  48.9 8.3 %shard_map.247 = (f32[256,512]{1,0:T(8,128)S(1)}, f32[256,128]{1,0:T(8,128)S(1)}, bf16[256,512]{1,0:T(8,128)(2,1)S(1)}, bf16[256,384]{1,0:T(8,128)(2,1)S(1)}, f3...) custom-call(s32[1]{0:T(128)} %bitcast.refs_0_, ...), custom_call_target="tpu_custom_call" | custom-call | flops 5000000000 | bytes 8000000 | tf_op jit(solution)/shard_map/pallas_call | solution.py:358
  58.3 5.5 %shard_map.248 = (f32[256,512]{1,0:T(8,128)S(1)}, f32[256,128]{1,0:T(8,128)S(1)}, bf16[256,512]{1,0:T(8,128)(2,1)S(1)}, f32[256,512]{1,0:T(8,128)S(1)}, f32[256,...) custom-call(s32[1]{0:T(128)} %bitcast.refs_0_, ...), custom_call_target="tpu_custom_call" | custom-call | flops 5000000000 | bytes 8000000 | tf_op jit(solution)/shard_map/pallas_call | solution.py:358
  66.2 5.1 %collective-permute-done.15.refs_6_ = bf16[208,512]{1,0:T(8,128)(2,1)S(1)} collective-permute-done((bf16[208,512]{1,0:T(8,128)(2,1)S(1)}, bf16[208,512]{1,0:T(8,128)(2,1)S(1)}, u32[]{:S(2)}, u32[]{:S(2)}) %collective-permute-start.15) | collective-permute-done | bytes 213024 | tf_op jit(solution)/shard_map/ppermute | solution.py:424
  74.8 6.3 %collective-permute-done.17 = bf16[196,512]{1,0:T(8,128)(2,1)} collective-permute-done((bf16[196,512]{1,0:T(8,128)(2,1)}, bf16[196,512]{1,0:T(8,128)(2,1)}, u32[]{:S(2)}, u32[]{:S(2)}) %collective-permute-start.17) | collective-permute-done | bytes 200736 | tf_op jit(solution)/shard_map/ppermute | solution.py:415
  81.1 16.7 %collective-permute-done.19 = bf16[208,512]{1,0:T(8,128)(2,1)S(1)} collective-permute-done((bf16[208,512]{1,0:T(8,128)(2,1)S(1)}, bf16[208,512]{1,0:T(8,128)(2,1)S(1)}, u32[]{:S(2)}, u32[]{:S(2)}) %collective-permute-start.19) | collective-permute-done | bytes 213024 | tf_op jit(solution)/shard_map/ppermute | solution.py:424
  102.2 13.2 %shard_map.250 = (bf16[4,256,512]{2,1,0:T(8,128)(2,1)}, f32[256,512]{1,0:T(8,128)S(1)}, bf16[256,512]{1,0:T(8,128)(2,1)S(1)}, f32[8,512]{1,0:T(8,128)S(1)}) custom-call(s32[1]{0:T(128)} %bitcast.refs_0_, f32[16,512]{1,0:T(8,128)S(1)} %concatenate.75.refs_1_, ...), custom_call_target="tpu_custom_call", output_to_operand_aliasing={{0}: (17, {}), {2}: (18, {}), {3}: (19, {})} | custom-call | flops 5000000000 | bytes 8000000 | tf_op jit(solution)/shard_map/pallas_call | solution.py:358
  119.6 9.6 %shard_map.251 = (f32[4,64,256]{2,1,0:T(8,128)S(1)}, bf16[4,256,384]{2,1,0:T(8,128)(2,1)}, f32[8,512]{1,0:T(8,128)S(1)}, bf16[208,512]{1,0:T(8,128)(2,1)S(1)}) custom-call(s32[1]{0:T(128)} %bitcast.refs_0_, f32[16,512]{1,0:T(8,128)S(1)} %concatenate.75.refs_1_, ...), custom_call_target="tpu_custom_call", output_to_operand_aliasing={{0}: (23, {}), {1}: (24, {}), {2}: (25, {}), {3}: (26, {})} | custom-call | flops 5000000000 | bytes 8000000 | tf_op jit(solution)/shard_map/pallas_call | solution.py:358
  135.7 2.6 convolution_bitcast_fusion
  142.8 2.8 %concatenate.91 = bf16[1,144,512]{2,1,0:T(8,128)(2,1)} concatenate(bf16[1,128,512]{2,1,0:T(8,128)(2,1)} %fusion.22, bf16[1,1,512]{2,1,0:T(2,128)(2,1)S(1)} %get-tuple-element.138, bf16[1,1,512]{2,1,0:T(2,128)(2,1)S(1)} %convert_bitcast_fusion.2, bf16[1,1,512]{2,1,0:T(2,128)(2,1)S(1)} %get-tuple-element.137, bf16[1,3,512]{2,1,0:T(4,128)(2,1)S(1)} %convert_bitcast_fusion, ...), dimensions={1} | concatenate | bytes 294912 | tf_op jit(solution)/shard_map/concatenate | solution.py:558
  162.8 4.4 %collective-permute-start.25 = (bf16[144,512]{1,0:T(8,128)(2,1)}, bf16[144,512]{1,0:T(8,128)(2,1)}, u32[]{:S(2)}, u32[]{:S(2)}) collective-permute-start(bf16[144,512]{1,0:T(8,128)(2,1)} %fusion.25), channel_id=1, source_target_pairs={{0,4},{12,8},{1,5},{13,9},{2,6},{14,10},{3,7},{15,11},{16,20},{28,... | collective-permute-start | bytes 442376 | tf_op jit(solution)/shard_map/ppermute | solution.py:433
  174.7 2.2 copy.57
  186.2 5.6 %collective-permute-done.29 = bf16[512,384]{1,0:T(8,128)(2,1)S(1)} collective-permute-done((bf16[512,384]{1,0:T(8,128)(2,1)S(1)}, bf16[512,384]{1,0:T(8,128)(2,1)S(1)}, u32[]{:S(2)}, u32[]{:S(2)}) %collective-permute-start.29) | collective-permute-done | bytes 393248 | tf_op jit(solution)/shard_map/ppermute | solution.py:415
  193.2 5.5 %collective-permute-start.30 = (bf16[512,384]{1,0:T(8,128)(2,1)S(1)}, bf16[512,384]{1,0:T(8,128)(2,1)S(1)}, u32[]{:S(2)}, u32[]{:S(2)}) collective-permute-start(bf16[512,384]{1,0:T(8,128)(2,1)S(1)} %fusion.10), channel_id=1, source_target_pairs={{0,4},{12,8},{1,5},{13,9},{2,6},{14,10},{3,7},{15,11},{16,20},{28,... | collective-permute-start | bytes 1179656 | tf_op jit(solution)/shard_map/ppermute | solution.py:433
  198.7 4.4 %collective-permute-done.39 = bf16[512,512]{1,0:T(8,128)(2,1)S(1)} collective-permute-done((bf16[512,512]{1,0:T(8,128)(2,1)S(1)}, bf16[512,512]{1,0:T(8,128)(2,1)S(1)}, u32[]{:S(2)}, u32[]{:S(2)}) %collective-permute-start.39) | collective-permute-done | bytes 524320 | tf_op jit(solution)/shard_map/ppermute | solution.py:415
  204.5 5.6 %collective-permute-start.40 = (bf16[512,512]{1,0:T(8,128)(2,1)S(1)}, bf16[512,512]{1,0:T(8,128)(2,1)S(1)}, u32[]{:S(2)}, u32[]{:S(2)}) collective-permute-start(bf16[512,512]{1,0:T(8,128)(2,1)S(1)} %fusion.7), channel_id=1, source_target_pairs={{0,4},{12,8},{1,5},{13,9},{2,6},{14,10},{3,7},{15,11},{16,20},{28,... | collective-permute-start | bytes 1572872 | tf_op jit(solution)/shard_map/ppermute | solution.py:433
  210.0 3.0 %collective-permute-done.34 = bf16[512,512]{1,0:T(8,128)(2,1)S(1)} collective-permute-done((bf16[512,512]{1,0:T(8,128)(2,1)S(1)}, bf16[512,512]{1,0:T(8,128)(2,1)S(1)}, u32[]{:S(2)}, u32[]{:S(2)}) %collective-permute-start.34) | collective-permute-done | bytes 524320 | tf_op jit(solution)/shard_map/ppermute | solution.py:415
  214.4 4.3 %collective-permute-start.35 = (bf16[512,512]{1,0:T(8,128)(2,1)S(1)}, bf16[512,512]{1,0:T(8,128)(2,1)S(1)}, u32[]{:S(2)}, u32[]{:S(2)}) collective-permute-start(bf16[512,512]{1,0:T(8,128)(2,1)S(1)} %fusion.5), channel_id=1, source_target_pairs={{0,4},{12,8},{1,5},{13,9},{2,6},{14,10},{3,7},{15,11},{16,20},{28,... | collective-permute-start | bytes 1572872 | tf_op jit(solution)/shard_map/ppermute | solution.py:433
  223.2 4.7 %collective-permute-done.35 = bf16[512,512]{1,0:T(8,128)(2,1)S(1)} collective-permute-done((bf16[512,512]{1,0:T(8,128)(2,1)S(1)}, bf16[512,512]{1,0:T(8,128)(2,1)S(1)}, u32[]{:S(2)}, u32[]{:S(2)}) %collective-permute-start.35) | collective-permute-done | bytes 524320 | tf_op jit(solution)/shard_map/ppermute | solution.py:433
  238.6 23.1 %collective-permute-done.42 = bf16[512,512]{1,0:T(8,128)(2,1)S(1)} collective-permute-done((bf16[512,512]{1,0:T(8,128)(2,1)S(1)}, bf16[512,512]{1,0:T(8,128)(2,1)S(1)}, u32[]{:S(2)}, u32[]{:S(2)}) %collective-permute-start.42) | collective-permute-done | bytes 524320 | tf_op jit(solution)/shard_map/ppermute | solution.py:435
  262.7 5.3 %collective-permute-done.37 = bf16[512,512]{1,0:T(8,128)(2,1)S(1)} collective-permute-done((bf16[512,512]{1,0:T(8,128)(2,1)S(1)}, bf16[512,512]{1,0:T(8,128)(2,1)S(1)}, u32[]{:S(2)}, u32[]{:S(2)}) %collective-permute-start.37) | collective-permute-done | bytes 524320 | tf_op jit(solution)/shard_map/ppermute | solution.py:435
  (280 shorter events, 107.9 us)
Async XLA Ops:
  3.1 15.8 %collective-permute-start.1 = (f32[4,512]{1,0:T(4,128)S(1)}, f32[4,512]{1,0:T(4,128)S(1)}, u32[]{:S(2)}, u32[]{:S(2)}) collective-permute-start(f32[4,512]{1,0:T(4,128)S(1)} %pad_maximum_fusion.6), channel_id=1, source_target_pairs={{0,2},{1,3},{2,0},{3,1},{4,6},{5,7},{6,4},{7,5},{8,10},{9,11},{10,... | collective-permute-start | bytes 24584 | tf_op jit(solution)/shard_map/ppermute | solution.py:415
  6.1 24.8 %collective-permute-start.5 = (bf16[3,512,128]{2,1,0:T(8,128)(2,1)}, bf16[3,512,128]{2,1,0:T(8,128)(2,1)}, u32[]{:S(2)}, u32[]{:S(2)}) collective-permute-start(bf16[3,512,128]{2,1,0:T(8,128)(2,1)} %bitcast.243), channel_id=1, source_target_pairs={{0,2},{1,3},{2,0},{3,1},{4,6},{5,7},{6,4},{7,5},{8,10},{9,11},{10,... | collective-permute-start | bytes 1179656 | tf_op jit(solution)/shard_map/ppermute | solution.py:415
  6.3 26.9 %collective-permute-start.3 = (bf16[3,512,128]{2,1,0:T(8,128)(2,1)}, bf16[3,512,128]{2,1,0:T(8,128)(2,1)}, u32[]{:S(2)}, u32[]{:S(2)}) collective-permute-start(bf16[3,512,128]{2,1,0:T(8,128)(2,1)} %bitcast.244), channel_id=1, source_target_pairs={{0,1},{1,0},{2,3},{3,2},{4,5},{5,4},{6,7},{7,6},{8,9},{9,8},{10,11... | collective-permute-start | bytes 1179656 | tf_op jit(solution)/shard_map/ppermute | solution.py:415
  6.7 15.8 %collective-permute-start.6 = (bf16[128,512]{1,0:T(8,128)(2,1)}, bf16[128,512]{1,0:T(8,128)(2,1)S(1)}, u32[]{:S(2)}, u32[]{:S(2)}) collective-permute-start(bf16[128,512]{1,0:T(8,128)(2,1)} %bitcast.248), channel_id=1, source_target_pairs={{0,2},{1,3},{2,0},{3,1},{4,6},{5,7},{6,4},{7,5},{8,10},{9,11},{10,... | collective-permute-start | bytes 393224 | tf_op jit(solution)/shard_map/ppermute | solution.py:415
  20.5 23.6 %collective-permute-start.12 = (bf16[512,512]{1,0:T(8,128)(2,1)S(1)}, bf16[512,512]{1,0:T(8,128)(2,1)}, u32[]{:S(2)}, u32[]{:S(2)}) collective-permute-start(bf16[512,512]{1,0:T(8,128)(2,1)S(1)} %bitcast.238), channel_id=1, source_target_pairs={{0,2},{1,3},{2,0},{3,1},{4,6},{5,7},{6,4},{7,5},{8,10},{9,11},{10,... | collective-permute-start | bytes 1572872 | tf_op jit(solution)/shard_map/ppermute | solution.py:415
  32.7 24.5 %collective-permute-start.10 = (bf16[512,512]{1,0:T(8,128)(2,1)S(1)}, bf16[512,512]{1,0:T(8,128)(2,1)}, u32[]{:S(2)}, u32[]{:S(2)}) collective-permute-start(bf16[512,512]{1,0:T(8,128)(2,1)S(1)} %bitcast.239), channel_id=1, source_target_pairs={{0,1},{1,0},{2,3},{3,2},{4,5},{5,4},{6,7},{7,6},{8,9},{9,8},{10,11... | collective-permute-start | bytes 1572872 | tf_op jit(solution)/shard_map/ppermute | solution.py:415
  33.2 24.0 %collective-permute-start.9 = (bf16[512,512]{1,0:T(8,128)(2,1)S(1)}, bf16[512,512]{1,0:T(8,128)(2,1)}, u32[]{:S(2)}, u32[]{:S(2)}) collective-permute-start(bf16[512,512]{1,0:T(8,128)(2,1)S(1)} %bitcast.234), channel_id=1, source_target_pairs={{0,1},{1,0},{2,3},{3,2},{4,5},{5,4},{6,7},{7,6},{8,9},{9,8},{10,11... | collective-permute-start | bytes 1572872 | tf_op jit(solution)/shard_map/ppermute | solution.py:415
  33.9 23.4 %collective-permute-start.13 = (bf16[512,512]{1,0:T(8,128)(2,1)}, bf16[512,512]{1,0:T(8,128)(2,1)}, u32[]{:S(2)}, u32[]{:S(2)}) collective-permute-start(bf16[512,512]{1,0:T(8,128)(2,1)} %collective-permute-done.11.refs_8_.refs_19_.refs_7_), channel_id=1, source_target_pairs={{0,1},{1,0},{2,3},{3,2},{4,5},{5,4},{6,7},{7,6},{8,9},{9,8},{10,11... | collective-permute-start | bytes 1572872 | tf_op jit(solution)/shard_map/ppermute | solution.py:415
  71.7 26.0 %collective-permute-start.19 = (bf16[208,512]{1,0:T(8,128)(2,1)S(1)}, bf16[208,512]{1,0:T(8,128)(2,1)S(1)}, u32[]{:S(2)}, u32[]{:S(2)}) collective-permute-start(bf16[208,512]{1,0:T(8,128)(2,1)S(1)} %get-tuple-element.61.refs_26_), channel_id=1, source_target_pairs={{16,0},{17,1},{18,2},{19,3},{20,4},{21,5},{22,6},{23,7},{24,8},{25... | collective-permute-start | bytes 638984 | tf_op jit(solution)/shard_map/ppermute | solution.py:424
  74.7 84.7 %collective-permute-start.16 = (bf16[196,512]{1,0:T(8,128)(2,1)}, bf16[196,512]{1,0:T(8,128)(2,1)}, u32[]{:S(2)}, u32[]{:S(2)}) collective-permute-start(bf16[196,512]{1,0:T(8,128)(2,1)} %get-tuple-element.136), channel_id=1, source_target_pairs={{0,1},{1,0},{2,3},{3,2},{4,5},{5,4},{6,7},{7,6},{8,9},{9,8},{10,11... | collective-permute-start | bytes 602120 | tf_op jit(solution)/shard_map/ppermute | solution.py:415
  81.1 81.3 %collective-permute-start.18 = (bf16[196,512]{1,0:T(8,128)(2,1)}, bf16[196,512]{1,0:T(8,128)(2,1)}, u32[]{:S(2)}, u32[]{:S(2)}) collective-permute-start(bf16[196,512]{1,0:T(8,128)(2,1)} %collective-permute-done.17), channel_id=1, source_target_pairs={{0,1},{1,0},{2,3},{3,2},{4,5},{5,4},{6,7},{7,6},{8,9},{9,8},{10,11... | collective-permute-start | bytes 602120 | tf_op jit(solution)/shard_map/ppermute | solution.py:415
  134.1 25.3 %collective-permute-start.21 = (bf16[196,512]{1,0:T(8,128)(2,1)}, bf16[196,512]{1,0:T(8,128)(2,1)}, u32[]{:S(2)}, u32[]{:S(2)}) collective-permute-start(bf16[196,512]{1,0:T(8,128)(2,1)} %get-tuple-element.134), channel_id=1, source_target_pairs={{0,2},{1,3},{2,0},{3,1},{4,6},{5,7},{6,4},{7,5},{8,10},{9,11},{10,... | collective-permute-start | bytes 602120 | tf_op jit(solution)/shard_map/ppermute | solution.py:415
  134.4 28.4 %collective-permute-start.20 = (bf16[196,512]{1,0:T(8,128)(2,1)}, bf16[196,512]{1,0:T(8,128)(2,1)}, u32[]{:S(2)}, u32[]{:S(2)}) collective-permute-start(bf16[196,512]{1,0:T(8,128)(2,1)} %get-tuple-element.134), channel_id=1, source_target_pairs={{0,1},{1,0},{2,3},{3,2},{4,5},{5,4},{6,7},{7,6},{8,9},{9,8},{10,11... | collective-permute-start | bytes 602120 | tf_op jit(solution)/shard_map/ppermute | solution.py:415
  159.4 21.9 %collective-permute-start.38 = (bf16[2,512,512]{2,1,0:T(8,128)(2,1)}, bf16[2,512,512]{2,1,0:T(8,128)(2,1)}, u32[]{:S(2)}, u32[]{:S(2)}) collective-permute-start(bf16[2,512,512]{2,1,0:T(8,128)(2,1)} %pad_maximum_fusion.1), channel_id=1, source_target_pairs={{0,1},{1,0},{2,3},{3,2},{4,5},{5,4},{6,7},{7,6},{8,9},{9,8},{10,11... | collective-permute-start | bytes 3145736 | tf_op jit(solution)/shard_map/ppermute | solution.py:415
  159.4 19.0 %collective-permute-start.28 = (bf16[2,512,384]{2,1,0:T(8,128)(2,1)}, bf16[2,512,384]{2,1,0:T(8,128)(2,1)}, u32[]{:S(2)}, u32[]{:S(2)}) collective-permute-start(bf16[2,512,384]{2,1,0:T(8,128)(2,1)} %pad_maximum_fusion.4), channel_id=1, source_target_pairs={{0,1},{1,0},{2,3},{3,2},{4,5},{5,4},{6,7},{7,6},{8,9},{9,8},{10,11... | collective-permute-start | bytes 2359304 | tf_op jit(solution)/shard_map/ppermute | solution.py:415
  162.3 21.0 %collective-permute-start.33 = (bf16[2,512,512]{2,1,0:T(8,128)(2,1)}, bf16[2,512,512]{2,1,0:T(8,128)(2,1)}, u32[]{:S(2)}, u32[]{:S(2)}) collective-permute-start(bf16[2,512,512]{2,1,0:T(8,128)(2,1)} %pad_maximum_fusion), channel_id=1, source_target_pairs={{0,1},{1,0},{2,3},{3,2},{4,5},{5,4},{6,7},{7,6},{8,9},{9,8},{10,11... | collective-permute-start | bytes 3145736 | tf_op jit(solution)/shard_map/ppermute | solution.py:415
  177.0 42.6 %collective-permute-start.27 = (bf16[144,512]{1,0:T(8,128)(2,1)S(1)}, bf16[144,512]{1,0:T(8,128)(2,1)S(1)}, u32[]{:S(2)}, u32[]{:S(2)}) collective-permute-start(bf16[144,512]{1,0:T(8,128)(2,1)S(1)} %add.93), channel_id=1, source_target_pairs={{4,0},{8,12},{5,1},{9,13},{6,2},{10,14},{7,3},{11,15},{20,16},{24,... | collective-permute-start | bytes 442376 | tf_op jit(solution)/shard_map/ppermute | solution.py:435
  182.7 20.4 %collective-permute-start.39 = (bf16[512,512]{1,0:T(8,128)(2,1)S(1)}, bf16[512,512]{1,0:T(8,128)(2,1)S(1)}, u32[]{:S(2)}, u32[]{:S(2)}) collective-permute-start(bf16[512,512]{1,0:T(8,128)(2,1)S(1)} %fusion.8), channel_id=1, source_target_pairs={{0,2},{1,3},{2,0},{3,1},{4,6},{5,7},{6,4},{7,5},{8,10},{9,11},{10,... | collective-permute-start | bytes 1572872 | tf_op jit(solution)/shard_map/ppermute | solution.py:415
  184.7 28.4 %collective-permute-start.34 = (bf16[512,512]{1,0:T(8,128)(2,1)S(1)}, bf16[512,512]{1,0:T(8,128)(2,1)S(1)}, u32[]{:S(2)}, u32[]{:S(2)}) collective-permute-start(bf16[512,512]{1,0:T(8,128)(2,1)S(1)} %fusion.6), channel_id=1, source_target_pairs={{0,2},{1,3},{2,0},{3,1},{4,6},{5,7},{6,4},{7,5},{8,10},{9,11},{10,... | collective-permute-start | bytes 1572872 | tf_op jit(solution)/shard_map/ppermute | solution.py:415
  193.2 25.6 %collective-permute-start.30 = (bf16[512,384]{1,0:T(8,128)(2,1)S(1)}, bf16[512,384]{1,0:T(8,128)(2,1)S(1)}, u32[]{:S(2)}, u32[]{:S(2)}) collective-permute-start(bf16[512,384]{1,0:T(8,128)(2,1)S(1)} %fusion.10), channel_id=1, source_target_pairs={{0,4},{12,8},{1,5},{13,9},{2,6},{14,10},{3,7},{15,11},{16,20},{28,... | collective-permute-start | bytes 1179656 | tf_op jit(solution)/shard_map/ppermute | solution.py:433
  204.5 17.2 %collective-permute-start.40 = (bf16[512,512]{1,0:T(8,128)(2,1)S(1)}, bf16[512,512]{1,0:T(8,128)(2,1)S(1)}, u32[]{:S(2)}, u32[]{:S(2)}) collective-permute-start(bf16[512,512]{1,0:T(8,128)(2,1)S(1)} %fusion.7), channel_id=1, source_target_pairs={{0,4},{12,8},{1,5},{13,9},{2,6},{14,10},{3,7},{15,11},{16,20},{28,... | collective-permute-start | bytes 1572872 | tf_op jit(solution)/shard_map/ppermute | solution.py:433
  220.3 15.7 %collective-permute-start.32 = (bf16[512,384]{1,0:T(8,128)(2,1)S(1)}, bf16[512,384]{1,0:T(8,128)(2,1)S(1)}, u32[]{:S(2)}, u32[]{:S(2)}) collective-permute-start(bf16[512,384]{1,0:T(8,128)(2,1)S(1)} %add.98), channel_id=1, source_target_pairs={{4,0},{8,12},{5,1},{9,13},{6,2},{10,14},{7,3},{11,15},{20,16},{24,... | collective-permute-start | bytes 1179656 | tf_op jit(solution)/shard_map/ppermute | solution.py:435
  232.6 29.0 %collective-permute-start.42 = (bf16[512,512]{1,0:T(8,128)(2,1)S(1)}, bf16[512,512]{1,0:T(8,128)(2,1)S(1)}, u32[]{:S(2)}, u32[]{:S(2)}) collective-permute-start(bf16[512,512]{1,0:T(8,128)(2,1)S(1)} %add.108), channel_id=1, source_target_pairs={{4,0},{8,12},{5,1},{9,13},{6,2},{10,14},{7,3},{11,15},{20,16},{24,... | collective-permute-start | bytes 1572872 | tf_op jit(solution)/shard_map/ppermute | solution.py:435
  236.3 31.7 %collective-permute-start.37 = (bf16[512,512]{1,0:T(8,128)(2,1)S(1)}, bf16[512,512]{1,0:T(8,128)(2,1)S(1)}, u32[]{:S(2)}, u32[]{:S(2)}) collective-permute-start(bf16[512,512]{1,0:T(8,128)(2,1)S(1)} %add.103), channel_id=1, source_target_pairs={{4,0},{8,12},{5,1},{9,13},{6,2},{10,14},{7,3},{11,15},{20,16},{24,... | collective-permute-start | bytes 1572872 | tf_op jit(solution)/shard_map/ppermute | solution.py:435
  (60 other events, 489.0 us)
